TPU v7x, 512 devices: a whole 4x4x16 slice. The times are simulated.
512 devices in a mesh: dp: 8 (over y, core), node: 64 (over z, x).
Axes of the slice: x: 4, y: 4, z: 16, core: 2. Of those that a mesh axis runs over, the one named last changes fastest.
Arguments:
- leaf_logp: float32 [128, 32, 1024], P('node', None, 'dp'), may hold values from -108 to 0, as said below
- weights: bfloat16 [128, 32, 1024], P('node'), may hold values from 0.0099487305 to 1
- upper_flows: float32 [128, 32, 1024], P('node', None, 'dp'), may hold values from 0.01 to 1
- leaf_asks: int32 [64, 64], P('node'), may hold values from 0 to 1
- prod_asks: int32 [64, 64], P('node'), may hold values from 0 to 1
- prod_child: int32 [128, 8], P('node'), may hold values from 0 to 63
- prod_valid: int32 [128, 8], P('node'), may hold values 0 or 1
- sum_child: int32 [128, 32], P('node'), may hold values from 0 to 63
- sum_valid: int32 [128, 32], P('node'), may hold values from 0 to 1, as said below
Outputs:
- sum_loglik: float32 [128, 32, 1024], P('node', None, 'dp')
- weight_flows: float32 [128, 32, 1024], P('node', None, 'dp')
- prod_flows: float32 [128, 32, 1024], P('node', None, 'dp')
Inputs may be any that keep to these rules, and one draw needn't show every extreme that they name: `leaf_logp`: log-probabilities, so no entry is positive. `leaf_asks`: entry (d, o) is which of owner o's 2 blocks device d reads. `prod_asks`: entry (d, o) is which of owner o's 2 blocks device d reads. `sum_valid`: the first child slot of every sum block is valid.
All inputs are finite; a program needn't handle non-finite values. No bound on the sum of `prod_valid` on one device may be relied on, other than what follows from the above.
Results may differ from a plain program's by a relative error of at most 0.0022.
Values sent between devices are 32-bit elements; how exact they have to be, the bound alone decides.
A program may use at most 64 MiB of HBM per device.

v0:
```python
import jax
import jax.numpy as jnp
from jax import lax
from jax.sharding import PartitionSpec as P


def local(
    leaf_logp,
    weights,
    upper_flows,
    leaf_asks,
    prod_asks,
    prod_child,
    prod_valid,
    sum_child,
    sum_valid,
):
    block_count, node_width, tok_count = leaf_logp.shape
    owners = lax.axis_size("node")
    slot_iota = jnp.arange(owners, dtype=jnp.int32)
    block_iota = jnp.arange(block_count, dtype=jnp.int32)
    exact = lax.Precision.HIGHEST
    asked = (
        lax.all_to_all(
            leaf_asks.reshape(owners, 1), "node", split_axis=0, concat_axis=0, tiled=True
        ),
        lax.all_to_all(
            prod_asks.reshape(owners, 1), "node", split_axis=0, concat_axis=0, tiled=True
        ),
    )
    ask_rows = (leaf_asks[0], prod_asks[0])

    def fetch_blocks(layer_vals, which_ask):
        whole_layer = lax.all_gather(layer_vals, "node", axis=0, tiled=True)
        return whole_layer[slot_iota * block_count + ask_rows[which_ask]]

    leaf_slots = fetch_blocks(leaf_logp, 0)
    mix_count = jnp.sum(
        (prod_child[:, :, None] == slot_iota[None, None, :]) * prod_valid[:, :, None], axis=1
    ).astype(jnp.float32)
    products = jnp.einsum("bo,okt->bkt", mix_count, leaf_slots, precision=exact)
    prod_slots = fetch_blocks(products, 1)
    picked = prod_slots[sum_child]
    is_valid = (sum_valid > 0)[:, :, None, None]
    col_max = jnp.max(jnp.where(is_valid, picked, -jnp.inf), axis=(1, 2))
    scaled = jnp.where(is_valid, jnp.exp(picked - col_max[:, None, None, :]), 0.0).astype(
        jnp.bfloat16
    )
    edges = picked.shape[1]
    flat_rows = scaled.reshape(block_count, edges * node_width, tok_count)
    totals = jnp.einsum("bkj,bjt->bkt", weights, flat_rows, preferred_element_type=jnp.float32)
    sum_loglik = jnp.log(totals) + col_max[:, None, :]
    ratios = (upper_flows / totals).astype(jnp.bfloat16)
    partial_counts = jnp.einsum(
        "bkt,bjt->bkj", ratios, flat_rows, preferred_element_type=jnp.float32
    )
    summed_counts = lax.psum_scatter(partial_counts, "dp", scatter_dimension=2, tiled=True)
    share_cols = summed_counts.shape[2]
    col_start = lax.axis_index("dp") * share_cols
    weight_cols = lax.dynamic_slice_in_dim(weights, col_start, share_cols, 2).astype(jnp.float32)
    weight_flows = weight_cols * summed_counts / (tok_count * lax.axis_size("dp"))
    spread_back = jnp.einsum("bkj,bkt->bjt", weights, ratios, preferred_element_type=jnp.float32)
    child_flows = (flat_rows.astype(jnp.float32) * spread_back).reshape(
        block_count, edges, node_width, tok_count
    )
    routing = (sum_child[:, :, None] == slot_iota[None, None, :]).astype(jnp.float32)
    slot_flows = jnp.einsum("beo,bekt->okt", routing, child_flows, precision=exact)
    returned = lax.all_to_all(slot_flows, "node", split_axis=0, concat_axis=0, tiled=True)
    pick_block = (asked[1][:, 0][:, None] == block_iota[None, :]).astype(jnp.float32)
    prod_flows = jnp.einsum("cb,ckt->bkt", pick_block, returned, precision=exact)
    return (sum_loglik, weight_flows, prod_flows)


def solution(mesh):
    in_specs = (
        P("node", None, "dp"),
        P("node", None, None),
        P("node", None, "dp"),
        P("node", None),
        P("node", None),
        P("node", None),
        P("node", None),
        P("node", None),
        P("node", None),
    )
    out_specs = (P("node", None, "dp"), P("node", None, "dp"), P("node", None, "dp"))
    return jax.shard_map(local, mesh=mesh, in_specs=in_specs, out_specs=out_specs, check_vma=False)
```

profile of v0, /device:TPU:2, one launch (start us, length us, event | category | flops | bytes accessed | tf_op | source)
XLA Modules:
  0.0 369.7 jit_solution(18280250931427675096)
XLA Ops:
  7.2 0.0 copy-start.3
  7.2 0.0 copy-start.2
  7.2 0.0 copy-start.4
  7.2 0.0 all-gather.3.cloned.1.call-start
  7.2 0.7 all-gather.3.cloned.1.call-update
  7.9 0.0 all-gather.5.cloned.1.call-start
  8.0 0.7 fusion.14
  8.6 0.8 select_reduce_fusion.1
  9.4 145.9 %all-gather.3.cloned.1.call-done = f32[128,32,128]{2,1,0:T(8,128)} async-done(((f32[2,32,128]{2,1,0:T(8,128)}), f32[128,32,128]{2,1,0:T(8,128)}) %all-gather.3.cloned.1.call-update) | async-done | bytes 2097168 | tf_op jit(solution)/shard_map/all_gather | solution.py:34
  155.3 2.2 gather_fusion
  157.5 1.2 fusion.4
  158.7 0.6 copy.46
  159.3 0.0 all-gather.5.cloned.1.call-update
  159.3 0.0 copy-done.3
  159.3 0.7 copy.50
  160.0 11.5 %all-to-all-start = ((s32[64,1,1]{2,1,0:T(1,128)}), s32[64,1,1]{2,1,0:T(1,128)S(1)}, u32[]{:S(2)}, u32[]{:S(2)}) async-start(s32[64,1,1]{2,1,0:T(1,128)} %copy.50), calls=%async_computation.1 | async-start | bytes 65536 | tf_op jit(solution)/shard_map/all_to_all | solution.py:27
  171.5 0.0 copy-done.2
  171.5 0.1 reshape.88
  171.6 0.0 copy-done.4
  171.6 0.1 broadcast_in_dim.38
  171.7 0.1 broadcast_in_dim.39
  171.9 124.6 %all-gather.5.cloned.1.call-done = f32[128,32,128]{2,1,0:T(8,128)} async-done(((f32[2,32,128]{2,1,0:T(8,128)}), f32[128,32,128]{2,1,0:T(8,128)}) %all-gather.5.cloned.1.call-update) | async-done | bytes 2097168 | tf_op jit(solution)/shard_map/all_gather | solution.py:34
  296.4 2.2 gather_fusion.1
  298.6 0.6 gather_fusion.2
  299.3 0.2 select_reduce_fusion
  299.5 0.0 copy-start
  299.5 0.0 copy-start.1
  299.5 0.3 copy.47
  299.8 0.2 select_convert_fusion
  300.0 0.3 copy-done
  300.4 0.0 copy-done.1
  300.4 0.9 divide_convert_fusion
  301.3 0.3 fusion
  301.6 0.3 copy.51
  302.0 1.3 convolution_bitcast_fusion
  303.3 1.6 copy.53
  304.9 0.0 all-to-all-done
  304.9 11.5 %all-to-all-start.1 = ((f32[64,32,128]{2,1,0:T(8,128)}), f32[64,32,128]{2,1,0:T(8,128)S(1)}, u32[]{:S(2)}, u32[]{:S(2)}) async-start(f32[64,32,128]{2,1,0:T(8,128)} %copy.53), calls=%async_computation.2 | async-start | bytes 2097152 | tf_op jit(solution)/shard_map/all_to_all | solution.py:68
  316.4 0.0 reduce-scatter.2.cloned.1.call-start
  316.4 0.9 fusion.17
  317.3 0.0 reduce-scatter.2.cloned.1.call-update
  317.4 1.2 reduce
  318.6 41.0 %reduce-scatter.2.cloned.1.call-done = f32[2,32,128]{2,1,0:T(8,128)} async-done(((f32[2,32,1024]{2,1,0:T(8,128)}), f32[2,32,128]{2,1,0:T(8,128)}) %reduce-scatter.2.cloned.1.call-update) | async-done | bytes 32784 | tf_op jit(solution)/shard_map/reduce_scatter | solution.py:57
  359.5 1.4 multiply_multiply_fusion
  360.9 0.5 all-to-all-done.1
  361.5 1.0 fusion.1
  362.5 0.6 copy.55
  (6 shorter events, 0.0 us)
Async XLA Ops:
  7.2 152.2 %copy-start.3 = (s32[1,64]{1,0:T(1,128)S(1)}, s32[1,64]{1,0:T(1,128)}, u32[]{:S(2)}) copy-start(s32[1,64]{1,0:T(1,128)} %param.13) | copy-start | bytes 772
  7.2 164.4 %copy-start.2 = (s32[2,32]{1,0:T(2,128)S(1)}, s32[2,32]{1,0:T(2,128)}, u32[]{:S(2)}) copy-start(s32[2,32]{1,0:T(2,128)} %param.16) | copy-start | bytes 772
  7.2 164.4 %copy-start.4 = (s32[2,32]{1,0:T(2,128)S(1)}, s32[2,32]{1,0:T(2,128)}, u32[]{:S(2)}) copy-start(s32[2,32]{1,0:T(2,128)} %param.17) | copy-start | bytes 772
  7.2 148.1 %all-gather.3.cloned.1.call-start = ((), (), s32[]{:S(2)}) async-start(), calls=%async_computation.3 | async-start | bytes 2129920 | tf_op jit(solution)/shard_map/all_gather | solution.py:34
  7.9 288.5 %all-gather.5.cloned.1.call-start = ((), (), s32[]{:S(2)}) async-start(), calls=%async_computation.4 | async-start | bytes 2129920 | tf_op jit(solution)/shard_map/all_gather | solution.py:34
  160.0 144.8 %all-to-all-start = ((s32[64,1,1]{2,1,0:T(1,128)}), s32[64,1,1]{2,1,0:T(1,128)S(1)}, u32[]{:S(2)}, u32[]{:S(2)}) async-start(s32[64,1,1]{2,1,0:T(1,128)} %copy.50), calls=%async_computation.1 | async-start | bytes 65536 | tf_op jit(solution)/shard_map/all_to_all | solution.py:27
  299.5 0.9 copy-start
  299.5 0.9 copy-start.1
  304.9 56.6 %all-to-all-start.1 = ((f32[64,32,128]{2,1,0:T(8,128)}), f32[64,32,128]{2,1,0:T(8,128)S(1)}, u32[]{:S(2)}, u32[]{:S(2)}) async-start(f32[64,32,128]{2,1,0:T(8,128)} %copy.53), calls=%async_computation.2 | async-start | bytes 2097152 | tf_op jit(solution)/shard_map/all_to_all | solution.py:68
  316.4 43.2 %reduce-scatter.2.cloned.1.call-start = ((), (), s32[]{:S(2)}) async-start(), calls=%async_computation.5 | async-start | bytes 294912 | tf_op jit(solution)/shard_map/reduce_scatter | solution.py:57
Sparse Core Ops, SparseCore 0:
  11.0 144.2 all-gather.2
  159.4 136.9 all-gather.4
  320.0 39.4 reduce-scatter.1
where the time goes:
time: 370 us
  waiting for transfers between devices  313 us (85%)
  starting transfers between devices  23.1 us (6%)
  between operations  13.9 us (4%)
  local copies, waits for them, and re-layouts  9.82 us (3%)
  matrix products  5.71 us (2%)
  other arithmetic  4.49 us (1%)
    all_gather x2, waiting for transfers between devices, fetch_blocks(): whole_layer = lax.all_gather(layer_vals, 'node', axis=0, tiled=True)  270 us
    reduce_scatter x1, waiting for transfers between devices, local(): lax.psum_scatter(partial_counts, 'dp', scatter_dimension=2, tiled=True)  41 us
    all_to_all x1, starting transfers between devices, local(): lax.all_to_all(prod_asks.reshape(owners, 1), 'node', split_axis=0, concat...  11.5 us
    all_to_all x1, starting transfers between devices, local(): lax.all_to_all(slot_flows, 'node', split_axis=0, concat_axis=0, tiled=True)  11.5 us
  transfers between devices with their start and end apart: 5, of which 4 were waited for; matrix products, arithmetic and copies ran while one was open for 4% of the time, Pallas kernels for 0%

commit v1 on v0

v1 whole, which is shorter than its diff:
```python
import jax
import jax.numpy as jnp
from jax import lax
from jax.experimental import pallas as pl
from jax.experimental.pallas import tpu as pltpu
from jax.sharding import PartitionSpec as P

Z, X, DP = 16, 4, 8
RA = 24
RB = 32 - RA
LANE = 64
MESH = pl.DeviceIdType.MESH
F32, I32, BF16 = jnp.float32, jnp.int32, jnp.bfloat16


def place(owner):
    return ((owner & 3) << 4) + (((owner >> 2) & 3) << 2) + (owner >> 4)


def place_of(z, x):
    return x * 16 + (z % 4) * 4 + z // 4


def kernel(
    leaf_h, w_h, upper_h, leaf_asks_h, prod_asks_h, prod_child_h, prod_valid_h, sum_child_h, sum_valid_h,
    loglik_o, wflow_o, pflow_o,
    w, upper, scol, prod_asks_v, leaf_asks, prod_asks, prod_child, prod_valid, sum_child, sum_valid, insem,
    lb, ib, tbl, wt, psel, scaled, spread, acc, slot, rx, dn, r1, s2, r2, cnt, rcnt,
    ib_s, tbl_s, lsem,
    a1s, a1r, a2s, a2r, axs, axr, b1s, b1r, bxs, bxr, bzs, bzr,
    i1s, i1r, ixs, ixr, izs, izr, cs, cr_, xs, xr_, z1s, z1r, z2s, z2r,
):
    node, dp = lax.axis_index("node"), lax.axis_index("dp")
    z, x = node // X, node % X
    zc, zq = z % 4, z // 4

    def nid(zz, xx):
        return lax.rem(zz + 2 * Z, Z) * X + lax.rem(xx + 2 * X, X)

    def pos(zz, xx):
        return place_of(lax.rem(zz + 2 * Z, Z), lax.rem(xx + 2 * X, X))

    def to(zz, xx):
        return {"node": nid(zz, xx)}

    me = pos(z, x)

    def own(p, n=1):
        return pl.ds(2 * p, 2 * n)

    loads = [
        pltpu.make_async_copy(src, dst, insem.at[i])
        for i, (src, dst) in enumerate((
            (leaf_asks_h, leaf_asks), (prod_asks_h, prod_asks), (prod_child_h, prod_child),
            (prod_valid_h, prod_valid), (prod_asks_h, prod_asks_v), (leaf_h, lb.at[own(me)]),
            (sum_child_h, sum_child), (sum_valid_h, sum_valid), (sum_child_h, scol), (w_h, w), (upper_h, upper),
        ))
    ]
    for c in loads:
        c.start()
    barrier = pltpu.get_barrier_semaphore()
    for d in (1, -1, -2, 4, -4, 8):
        pl.semaphore_signal(barrier, 1, device_id=to(z + d, x), device_id_type=MESH)
    for d in (1, 2, 3):
        pl.semaphore_signal(barrier, 1, device_id=to(z, x + d), device_id_type=MESH)
    for d in range(1, DP):
        pl.semaphore_signal(barrier, 1, device_id={"dp": lax.rem(dp + d, DP)}, device_id_type=MESH)

    sends = []

    def send(src, dst, s, r, dev):
        c = pltpu.make_async_remote_copy(src, dst, s, r, device_id=dev, device_id_type=MESH)
        c.start()
        sends.append(c)

    def recv(dst, sem):
        pltpu.make_async_copy(dst, dst, sem).wait()

    lb[128] = jnp.zeros((32, 128), F32)
    for c in loads[:5]:
        c.wait()
    lane = lax.broadcasted_iota(I32, (1, 128), 1)
    row = jnp.concatenate([prod_asks_v[...], jnp.zeros((1, 64), I32)], axis=1)
    for b in range(2):
        for e in range(8):
            c = prod_child[b, e]
            where = jnp.where(prod_valid[b, e] > 0, place(c) * 2 + leaf_asks[0, c], 128)
            row = jnp.where(lane == LANE + b * 8 + e, where, row)
    ib[me] = row

    loads[5].wait()
    pl.semaphore_wait(barrier, 16)

    FAR = ((0, 1), (2, 3), (1, 2))
    NEAR = ((0, 1), (1, -1), (2, 2))
    A = lambda p: lb.at[own(p), pl.ds(0, RA), :]
    for i, j in FAR:
        send(A(me), A(me), a1s.at[i], a1r.at[i], to(z + 4 * j, x))
    for i, j in FAR:
        v = lb.at[own(me), pl.ds(RA, RB), :]
        send(v, v, b1s.at[i], b1r.at[i], to(z + 4 * j, x))
    for i, j in FAR:
        send(ib.at[me], ib.at[me], i1s.at[i], i1r.at[i], to(z + 4 * j, x))
    for i, d in NEAR:
        send(A(me), A(me), a2s.at[i, 0], a2r.at[i, 0], to(z + d, x))
    for i in range(3):
        send(A(me), A(me), axs.at[i, 0], axr.at[i], to(z, x + i + 1))

    for c in loads[6:]:
        c.wait()
    c_row = jnp.concatenate([scol[0:1, :], scol[1:2, :]], axis=1)
    ri = lax.broadcasted_iota(I32, (64, 64), 0)
    ci = lax.broadcasted_iota(I32, (64, 64), 1)
    c_col = jnp.sum(jnp.where(ri == ci, c_row, 0), axis=1, keepdims=True)
    prev = jnp.max(jnp.where((c_col == c_row) & (ci < ri), ci, -1), axis=1, keepdims=True)
    last = jnp.max(jnp.where(c_row == ri, ci, -1), axis=1, keepdims=True)
    lanes = lax.broadcasted_iota(I32, (64, 128), 1)
    both = jnp.where(lanes == 0, prev, last)
    tbl[...] = jnp.where(both < 0, 64, both)
    tcopy = pltpu.make_async_copy(tbl, tbl_s, lsem.at[0])
    tcopy.start()

    for i, j in FAR:
        p = pos(z - 4 * j, x)
        recv(A(p), a1r.at[i])
        for n, d in NEAR:
            send(A(p), A(p), a2s.at[n, i + 1], a2r.at[n, i + 1], to(z + d, x))
        for n in range(3):
            send(A(p), A(p), axs.at[n, i + 1], axr.at[n], to(z, x + n + 1))
        recv(lb.at[own(p), pl.ds(RA, RB), :], b1r.at[i])
        recv(ib.at[p], i1r.at[i])

    def cls(xx, zz):
        return xx * 16 + (lax.rem(zz + Z, Z) % 4) * 4

    def Bc(xx, zz):
        return lb.at[own(cls(xx, zz), 4), pl.ds(RA, RB), :]

    def Ic(xx, zz):
        return ib.at[pl.ds(cls(xx, zz), 4)]

    for n in range(3):
        send(Bc(x, z), Bc(x, z), bxs.at[n], bxr.at[n], to(z, x + n + 1))
        send(Ic(x, z), Ic(x, z), ixs.at[n], ixr.at[n], to(z, x + n + 1))
    for n, d in NEAR:
        send(Bc(x, z), Bc(x, z), bzs.at[n, 0], bzr.at[n], to(z + d, x))
        send(Ic(x, z), Ic(x, z), izs.at[n, 0], izr.at[n], to(z + d, x))

    def onward(k):
        for n, d in NEAR:
            p = pos(z - d - 4 * k, x)
            recv(A(p), a2r.at[n, k])
            for m in range(3):
                send(A(p), A(p), axs.at[m, 4 + n * 4 + k], axr.at[m], to(z, x + m + 1))

    onward(0)
    onward(1)
    for n in range(3):
        xx = lax.rem(x + 3 - n, X)
        recv(Bc(xx, z), bxr.at[n])
        recv(Ic(xx, z), ixr.at[n])
        for m, d in NEAR:
            send(Bc(xx, z), Bc(xx, z), bzs.at[m, n + 1], bzr.at[m], to(z + d, x))
            send(Ic(xx, z), Ic(xx, z), izs.at[m, n + 1], izr.at[m], to(z + d, x))
    onward(3)
    onward(2)

    for b in range(2):
        wt[b] = jnp.transpose(w[b].astype(F32)).astype(BF16)

    for n in range(3):
        recv(ib.at[pl.ds(0, 16)], izr.at[n])
    icopy = pltpu.make_async_copy(ib, ib_s, lsem.at[1])
    icopy.start()
    acc[64] = jnp.zeros((32, 128), F32)
    tcopy.wait()
    icopy.wait()
    for n in range(3):
        recv(lb.at[own(0, 16), pl.ds(RA, RB), :], bzr.at[n])
        recv(lb.at[own(0, 16), pl.ds(0, RA), :], axr.at[n])

    for b in range(2):

        def product(e, top, b=b):
            c = sum_child[b, e]
            base = LANE + prod_asks[0, c] * 8
            pc = place(c)
            total = None
            for j in range(8):
                v = lb[ib_s[pc, 0, base + j]]
                total = v if total is None else total + v
            psel[b * 32 + e] = total
            high = jnp.maximum(jnp.maximum(total[0:8], total[8:16]), jnp.maximum(total[16:24], total[24:32]))
            return jnp.maximum(top, jnp.where(sum_valid[b, e] > 0, high, -jnp.inf))

        top = lax.fori_loop(0, 32, product, jnp.full((8, 128), -jnp.inf, F32))
        colmax = jnp.max(top, axis=0, keepdims=True)

        def scale(e, _, b=b, colmax=colmax):
            v = jnp.where(sum_valid[b, e] > 0, jnp.exp(psel[b * 32 + e] - colmax), 0.0)
            scaled[b, pl.ds(pl.multiple_of(e * 32, 32), 32), :] = v.astype(BF16)
            return 0

        lax.fori_loop(0, 32, scale, 0)
        totals = jnp.dot(w[b], scaled[b], preferred_element_type=F32)
        loglik_o[b] = jnp.log(totals) + colmax
        ratios = (upper[b] / totals).astype(BF16)
        counts = lax.dot_general(ratios, scaled[b], (((1,), (1,)), ((), ())), preferred_element_type=F32)
        for d in range(DP):
            cnt[d, b] = counts[:, d * 128 : (d + 1) * 128]
        spread[b] = jnp.dot(wt[b], ratios, preferred_element_type=F32)

    for d in range(1, DP):
        other = lax.rem(dp + d, DP)
        send(cnt.at[other], rcnt.at[d - 1], cs.at[d - 1], cr_.at[d - 1], {"dp": other})

    def flow(e, _, b):
        rows = pl.ds(pl.multiple_of(e * 32, 32), 32)
        i = b * 32 + e
        acc[i] = scaled[b, rows, :].astype(F32) * spread[b, rows, :] + acc[tbl_s[i, 0]]
        return 0

    for b in range(2):
        lax.fori_loop(0, 32, lambda e, _, b=b: flow(e, _, b), 0)

    def fill(t, _):
        xx = lax.rem(x + t // 16, X)
        zz = (t % 4) * 4 + lax.rem(z + (t // 4) % 4, 4)
        slot[t] = acc[tbl_s[zz * X + xx, 1]]
        return 0

    ORDER = (2, 1, 3, 0)
    lax.fori_loop(0, 64, fill, 0)
    for c in ORDER:
        for n in (1, 2, 3):
            src = slot.at[pl.ds(n * 16 + c * 4, 4)]
            send(src, rx.at[n - 1, c], xs.at[n - 1, c], xr_.at[n - 1, c], to(z, x + n))

    for c in ORDER:
        for n in range(3):
            recv(rx.at[n, c], xr_.at[n, c])

        def merge(q, _, c=c):
            o = (q * 4 + lax.rem(z + c, 4)) * X + x
            v = slot[c * 4 + q]
            zero = jnp.zeros_like(v)
            a = prod_asks[0, o]
            d0, d1 = jnp.where(a == 0, v, zero), jnp.where(a == 0, zero, v)
            for n in range(3):
                a = ib_s[pos(z, x + 3 - n), 0, o]
                v = rx[n, c, q]
                d0, d1 = d0 + jnp.where(a == 0, v, zero), d1 + jnp.where(a == 0, zero, v)
            dn[c, q, 0] = d0
            dn[c, q, 1] = d1
            return 0

        lax.fori_loop(0, 4, merge, 0)
        if c:
            i = {2: 2, 1: 0, 3: 1}[c]
            send(dn.at[c], r1.at[i], z1s.at[i], z1r.at[i], to(z + NEAR[i][1], x))

    for i in (2, 0, 1):
        recv(r1.at[i], z1r.at[i])
    for j in (2, 1, 3, 0):
        q = lax.rem(zq + j, 4)
        s2[j] = (dn[0, q] + r1[0, q]) + (r1[1, q] + r1[2, q])
        if j:
            send(s2.at[j], r2.at[j - 1], z2s.at[j - 1], z2r.at[j - 1], to(z + 4 * j, x))

    for d in range(DP - 1):
        recv(rcnt.at[d], cr_.at[d])
    for b in range(2):
        total = cnt[dp, b]
        for d in range(DP - 1):
            total = total + rcnt[d, b]
        columns = pl.ds(pl.multiple_of(dp * 128, 128), 128)
        wflow_o[b] = w[b, :, columns].astype(F32) * total * (1.0 / 1024)

    for j in (1, 3, 2):
        recv(r2.at[j - 1], z2r.at[j - 1])
    pflow_o[...] = (s2[0] + r2[0]) + (r2[1] + r2[2])
    for c in sends:
        c.wait_send()


def local(leaf_logp, weights, upper_flows, leaf_asks, prod_asks, prod_child, prod_valid, sum_child, sum_valid):
    D = pltpu.SemaphoreType.DMA
    block = jax.ShapeDtypeStruct((2, 32, 128), F32)
    vmem, hbm = pl.BlockSpec(memory_space=pltpu.VMEM), pl.BlockSpec(memory_space=pltpu.HBM)
    V, S = pltpu.VMEM, pltpu.SMEM
    return pl.pallas_call(
        kernel,
        out_shape=(block, block, block),
        in_specs=[hbm] * 9,
        out_specs=(vmem,) * 3,
        scratch_shapes=[
            V((2, 32, 1024), BF16),
            V((2, 32, 128), F32),
            V((2, 32), I32),
            V((1, 64), I32),
            S((1, 64), I32), S((1, 64), I32), S((2, 8), I32), S((2, 8), I32), S((2, 32), I32), S((2, 32), I32),
            D((11,)),
            V((129, 32, 128), F32),
            V((64, 1, 128), I32),
            V((64, 128), I32),
            V((2, 1024, 32), BF16),
            V((64, 32, 128), F32),
            V((2, 1024, 128), BF16),
            V((2, 1024, 128), F32),
            V((65, 32, 128), F32),
            V((64, 32, 128), F32),
            V((3, 4, 4, 32, 128), F32),
            V((4, 4, 2, 32, 128), F32),
            V((3, 4, 2, 32, 128), F32),
            V((4, 2, 32, 128), F32),
            V((3, 2, 32, 128), F32),
            V((8, 2, 32, 128), F32),
            V((7, 2, 32, 128), F32),
            pltpu.SMEM((64, 1, 128), I32),
            pltpu.SMEM((64, 128), I32),
            D((2,)),
            D((3,)), D((3,)),
            D((3, 4)), D((3, 4)),
            D((3, 16)), D((3,)),
            D((3,)), D((3,)),
            D((3,)), D((3,)),
            D((3, 4)), D((3,)),
            D((3,)), D((3,)),
            D((3,)), D((3,)),
            D((3, 4)), D((3,)),
            D((7,)), D((7,)),
            D((3, 4)), D((3, 4)),
            D((3,)), D((3,)),
            D((3,)), D((3,)),
        ],
        compiler_params=pltpu.CompilerParams(
            collective_id=0, has_side_effects=True, vmem_limit_bytes=63 * 2**20
        ),
        name="em_pass",
    )(
        leaf_logp, weights, upper_flows, leaf_asks, prod_asks, prod_child, prod_valid, sum_child, sum_valid
    )


def solution(mesh):
    tok, own = P("node", None, "dp"), P("node", None)
    return jax.shard_map(
        local,
        mesh=mesh,
        in_specs=(tok, P("node", None, None), tok, own, own, own, own, own, own),
        out_specs=(tok, tok, tok),
        check_vma=False,
    )
```

time: 370 us -> 77.1 us (0.21)
  the two profiles are of different devices: /device:TPU:2 before, /device:TPU:32 now
where the time goes in v1:
time: 77.1 us; the launch traced here: 76.9 us
  Pallas kernels  73.4 us (95%)
  local copies, waits for them, and re-layouts  2.77 us (4%)
    pallas_call x1, Pallas kernels, local(): pl.pallas_call(kernel, out_shape=(block, block, block), in_specs=[hbm] *...  73.4 us
    unnamed x7, local copies, waits for them, and re-layouts  2.77 us

profile of v1, /device:TPU:32, one launch (start us, length us, event | category | flops | bytes accessed | tf_op | source)
XLA Modules:
  0.0 76.9 jit_solution(11627168552428036581)
XLA Ops:
  0.6 73.4 %em_pass.1 = (f32[2,32,128]{2,1,0:T(8,128)}, f32[2,32,128]{2,1,0:T(8,128)}, f32[2,32,128]{2,1,0:T(8,128)}) custom-call(f32[2,32,128]{2,1,0:T(8,128)} %leaf_h.1, bf16[2,32,1024]{2,1,0:T(8,128)(2,1)} %w_h.1, f32[2,32,128]{2,1,0:T(8,128)} %upper_h.1, s32[1,64]{1,0:T(1,128)} %leaf_asks_h.1, s32[1,64]{1,0:T(1,128)} %prod_asks_h.1, s32[2,8]{1,0:T(2,128)} %prod_child_h.1, ...), custom_call_target="tpu_custom_call" | custom-call | tf_op jit(solution)/shard_map/em_pass/pallas_call | solution.py:291
  74.1 0.0 copy-start.1
  74.1 1.4 %copy.15 = f32[2,32,128]{2,1,0:T(8,128)} copy(f32[2,32,128]{2,1,0:T(8,128)} %get-tuple-element.6) | data formatting | bytes 65536
  75.5 0.0 copy-done.1
  75.5 0.0 copy-start
  75.5 0.6 copy.16
  76.1 0.2 copy-done
  76.2 0.6 copy.17
Async XLA Ops:
  74.1 1.4 %copy-start.1 = (f32[2,32,128]{2,1,0:T(8,128)S(1)}, f32[2,32,128]{2,1,0:T(8,128)}, u32[]{:S(2)}) copy-start(f32[2,32,128]{2,1,0:T(8,128)} %get-tuple-element.7) | copy-start | bytes 98308
  75.5 0.8 %copy-start = (f32[2,32,128]{2,1,0:T(8,128)S(1)}, f32[2,32,128]{2,1,0:T(8,128)}, u32[]{:S(2)}) copy-start(f32[2,32,128]{2,1,0:T(8,128)} %get-tuple-element.8) | copy-start | bytes 98308

commit v2 on v1

--- a/solution.py
+++ b/solution.py
@@ -8,6 +8,8 @@
 Z, X, DP = 16, 4, 8
 RA = 24
 RB = 32 - RA
+GROUPS = ((8, -6, 7, -7), (6, -4, 5, -5), (4, -2, 3, -3), (2, 0, 1, -1))
+PLUS, MINUS = (0, 3, 4, 12, 9, 11), (1, 8, 5, 13, 7, 15)
 LANE = 64
 MESH = pl.DeviceIdType.MESH
 F32, I32, BF16 = jnp.float32, jnp.int32, jnp.bfloat16
@@ -25,10 +27,10 @@
     leaf_h, w_h, upper_h, leaf_asks_h, prod_asks_h, prod_child_h, prod_valid_h, sum_child_h, sum_valid_h,
     loglik_o, wflow_o, pflow_o,
     w, upper, scol, prod_asks_v, leaf_asks, prod_asks, prod_child, prod_valid, sum_child, sum_valid, insem,
-    lb, ib, tbl, wt, psel, scaled, spread, acc, slot, rx, dn, r1, s2, r2, cnt, rcnt,
+    lb, ib, tbl, wt, psel, ratio, scaled, spread, acc, slot, rx, dn, near, up, usum, down, dsum, cnt, rcnt,
     ib_s, tbl_s, lsem,
-    a1s, a1r, a2s, a2r, axs, axr, b1s, b1r, bxs, bxr, bzs, bzr,
-    i1s, i1r, ixs, ixr, izs, izr, cs, cr_, xs, xr_, z1s, z1r, z2s, z2r,
+    a1s, a1r, a2s, a2r, axs, axr, px, mx, fr, b1s, b1r, bxs, bxr, bzs, bzr,
+    i1s, i1r, ixs, ixr, izs, izr, cs, cr_, xs, xr_, ns, nr, us, ur, ds_, dr,
 ):
     node, dp = lax.axis_index("node"), lax.axis_index("dp")
     z, x = node // X, node % X
@@ -47,6 +49,14 @@
 
     def own(p, n=1):
         return pl.ds(2 * p, 2 * n)
+
+    barrier = pltpu.get_barrier_semaphore()
+    for d in (1, -1, 2, -2, 4, -4, 8):
+        pl.semaphore_signal(barrier, 1, device_id=to(z + d, x), device_id_type=MESH)
+    for d in (1, 2, 3):
+        pl.semaphore_signal(barrier, 1, device_id=to(z, x + d), device_id_type=MESH)
+    for d in range(1, DP):
+        pl.semaphore_signal(barrier, 1, device_id={"dp": lax.rem(dp + d, DP)}, device_id_type=MESH)
 
     loads = [
         pltpu.make_async_copy(src, dst, insem.at[i])
@@ -58,14 +68,6 @@
     ]
     for c in loads:
         c.start()
-    barrier = pltpu.get_barrier_semaphore()
-    for d in (1, -1, -2, 4, -4, 8):
-        pl.semaphore_signal(barrier, 1, device_id=to(z + d, x), device_id_type=MESH)
-    for d in (1, 2, 3):
-        pl.semaphore_signal(barrier, 1, device_id=to(z, x + d), device_id_type=MESH)
-    for d in range(1, DP):
-        pl.semaphore_signal(barrier, 1, device_id={"dp": lax.rem(dp + d, DP)}, device_id_type=MESH)
-
     sends = []
 
     def send(src, dst, s, r, dev):
@@ -89,7 +91,7 @@
     ib[me] = row
 
     loads[5].wait()
-    pl.semaphore_wait(barrier, 16)
+    pl.semaphore_wait(barrier, 17)
 
     FAR = ((0, 1), (2, 3), (1, 2))
     NEAR = ((0, 1), (1, -1), (2, 2))
@@ -103,8 +105,29 @@
         send(ib.at[me], ib.at[me], i1s.at[i], i1r.at[i], to(z + 4 * j, x))
     for i, d in NEAR:
         send(A(me), A(me), a2s.at[i, 0], a2r.at[i, 0], to(z + d, x))
-    for i in range(3):
-        send(A(me), A(me), axs.at[i, 0], axr.at[i], to(z, x + i + 1))
+
+    def z_of(i):
+        return z - 4 * i if i < 4 else z - NEAR[(i - 4) // 4][1] - 4 * (i % 4)
+
+    def across(i):
+        v = A(pos(z_of(i), x))
+        send(v, v, axs.at[0, i], px.at[PLUS.index(i)] if i in PLUS else axr.at[0], to(z, x + 1))
+        send(v, v, axs.at[2, i], mx.at[MINUS.index(i)] if i in MINUS else axr.at[2], to(z, x - 1))
+        if i not in PLUS + MINUS:
+            send(v, v, axs.at[1, i], axr.at[1], to(z, x + 2))
+
+    def relay(*chunks):
+        for i in chunks:
+            if i in PLUS:
+                v = A(pos(z_of(i), x - 1))
+                recv(v, px.at[PLUS.index(i)])
+                send(v, v, axs.at[1, i], fr.at[0], to(z, x + 1))
+            else:
+                v = A(pos(z_of(i), x + 1))
+                recv(v, mx.at[MINUS.index(i)])
+                send(v, v, axs.at[1, i], fr.at[1], to(z, x - 1))
+
+    across(0)
 
     for c in loads[6:]:
         c.wait()
@@ -125,8 +148,9 @@
         recv(A(p), a1r.at[i])
         for n, d in NEAR:
             send(A(p), A(p), a2s.at[n, i + 1], a2r.at[n, i + 1], to(z + d, x))
-        for n in range(3):
-            send(A(p), A(p), axs.at[n, i + 1], axr.at[n], to(z, x + n + 1))
+        across(i + 1)
+        if i == 2:
+            relay(0)
         recv(lb.at[own(p), pl.ds(RA, RB), :], b1r.at[i])
         recv(ib.at[p], i1r.at[i])
 
@@ -150,11 +174,13 @@
         for n, d in NEAR:
             p = pos(z - d - 4 * k, x)
             recv(A(p), a2r.at[n, k])
-            for m in range(3):
-                send(A(p), A(p), axs.at[m, 4 + n * 4 + k], axr.at[m], to(z, x + m + 1))
+            across(4 + n * 4 + k)
 
     onward(0)
+    relay(1, 3)
     onward(1)
+    relay(4, 8, 12)
+    onward(3)
     for n in range(3):
         xx = lax.rem(x + 3 - n, X)
         recv(Bc(xx, z), bxr.at[n])
@@ -162,8 +188,9 @@
         for m, d in NEAR:
             send(Bc(xx, z), Bc(xx, z), bzs.at[m, n + 1], bzr.at[m], to(z + d, x))
             send(Ic(xx, z), Ic(xx, z), izs.at[m, n + 1], izr.at[m], to(z + d, x))
-    onward(3)
+    relay(5, 9, 13)
     onward(2)
+    relay(7, 11, 15)
 
     for b in range(2):
         wt[b] = jnp.transpose(w[b].astype(F32)).astype(BF16)
@@ -177,7 +204,11 @@
     icopy.wait()
     for n in range(3):
         recv(lb.at[own(0, 16), pl.ds(RA, RB), :], bzr.at[n])
-        recv(lb.at[own(0, 16), pl.ds(0, RA), :], axr.at[n])
+        recv(lb.at[own(0, (10, 4, 10)[n]), pl.ds(0, RA), :], axr.at[n])
+    for n in range(2):
+        recv(lb.at[own(0, 6), pl.ds(0, RA), :], fr.at[n])
+
+    gathered = len(sends)
 
     for b in range(2):
 
@@ -193,7 +224,7 @@
             high = jnp.maximum(jnp.maximum(total[0:8], total[8:16]), jnp.maximum(total[16:24], total[24:32]))
             return jnp.maximum(top, jnp.where(sum_valid[b, e] > 0, high, -jnp.inf))
 
-        top = lax.fori_loop(0, 32, product, jnp.full((8, 128), -jnp.inf, F32))
+        top = lax.fori_loop(0, 32, product, jnp.full((8, 128), -jnp.inf, F32), unroll=4)
         colmax = jnp.max(top, axis=0, keepdims=True)
 
         def scale(e, _, b=b, colmax=colmax):
@@ -201,71 +232,71 @@
             scaled[b, pl.ds(pl.multiple_of(e * 32, 32), 32), :] = v.astype(BF16)
             return 0
 
-        lax.fori_loop(0, 32, scale, 0)
+        lax.fori_loop(0, 32, scale, 0, unroll=4)
         totals = jnp.dot(w[b], scaled[b], preferred_element_type=F32)
         loglik_o[b] = jnp.log(totals) + colmax
         ratios = (upper[b] / totals).astype(BF16)
-        counts = lax.dot_general(ratios, scaled[b], (((1,), (1,)), ((), ())), preferred_element_type=F32)
+        ratio[b] = ratios
+        spread[b] = jnp.dot(wt[b], ratios, preferred_element_type=F32)
+
+    def flow(i, _):
+        rows = pl.ds(pl.multiple_of(i % 32 * 32, 32), 32)
+        b = i // 32
+        acc[i] = scaled[b, rows, :].astype(F32) * spread[b, rows, :] + acc[tbl_s[i, 0]]
+        return 0
+
+    lax.fori_loop(0, 64, flow, 0, unroll=4)
+
+    at_z = {d: lax.rem(z + d + Z, Z) for d in range(-7, 9)}
+    for g in range(4):
+        for n in range(4):
+            for k in range(4):
+                slot[n, g, k] = acc[tbl_s[at_z[GROUPS[g][k]] * X + lax.rem(x + n, X), 1]]
+        for n in (1, 2, 3):
+            send(slot.at[n, g], rx.at[n - 1, g], xs.at[n - 1, g], xr_.at[n - 1, g], to(z, x + n))
+
+    for b in range(2):
+        counts = lax.dot_general(ratio[b], scaled[b], (((1,), (1,)), ((), ())), preferred_element_type=F32)
         for d in range(DP):
             cnt[d, b] = counts[:, d * 128 : (d + 1) * 128]
-        spread[b] = jnp.dot(wt[b], ratios, preferred_element_type=F32)
-
     for d in range(1, DP):
         other = lax.rem(dp + d, DP)
         send(cnt.at[other], rcnt.at[d - 1], cs.at[d - 1], cr_.at[d - 1], {"dp": other})
 
-    def flow(e, _, b):
-        rows = pl.ds(pl.multiple_of(e * 32, 32), 32)
-        i = b * 32 + e
-        acc[i] = scaled[b, rows, :].astype(F32) * spread[b, rows, :] + acc[tbl_s[i, 0]]
-        return 0
-
-    for b in range(2):
-        lax.fori_loop(0, 32, lambda e, _, b=b: flow(e, _, b), 0)
-
-    def fill(t, _):
-        xx = lax.rem(x + t // 16, X)
-        zz = (t % 4) * 4 + lax.rem(z + (t // 4) % 4, 4)
-        slot[t] = acc[tbl_s[zz * X + xx, 1]]
-        return 0
-
-    ORDER = (2, 1, 3, 0)
-    lax.fori_loop(0, 64, fill, 0)
-    for c in ORDER:
-        for n in (1, 2, 3):
-            src = slot.at[pl.ds(n * 16 + c * 4, 4)]
-            send(src, rx.at[n - 1, c], xs.at[n - 1, c], xr_.at[n - 1, c], to(z, x + n))
-
-    for c in ORDER:
+    for c in sends[:gathered]:
+        c.wait_send()
+
+    peers_x = [pos(z, x + 3 - n) for n in range(3)]
+    for g in range(4):
         for n in range(3):
-            recv(rx.at[n, c], xr_.at[n, c])
-
-        def merge(q, _, c=c):
-            o = (q * 4 + lax.rem(z + c, 4)) * X + x
-            v = slot[c * 4 + q]
-            zero = jnp.zeros_like(v)
-            a = prod_asks[0, o]
-            d0, d1 = jnp.where(a == 0, v, zero), jnp.where(a == 0, zero, v)
-            for n in range(3):
-                a = ib_s[pos(z, x + 3 - n), 0, o]
-                v = rx[n, c, q]
-                d0, d1 = d0 + jnp.where(a == 0, v, zero), d1 + jnp.where(a == 0, zero, v)
-            dn[c, q, 0] = d0
-            dn[c, q, 1] = d1
-            return 0
-
-        lax.fori_loop(0, 4, merge, 0)
-        if c:
-            i = {2: 2, 1: 0, 3: 1}[c]
-            send(dn.at[c], r1.at[i], z1s.at[i], z1r.at[i], to(z + NEAR[i][1], x))
-
-    for i in (2, 0, 1):
-        recv(r1.at[i], z1r.at[i])
-    for j in (2, 1, 3, 0):
-        q = lax.rem(zq + j, 4)
-        s2[j] = (dn[0, q] + r1[0, q]) + (r1[1, q] + r1[2, q])
-        if j:
-            send(s2.at[j], r2.at[j - 1], z2s.at[j - 1], z2r.at[j - 1], to(z + 4 * j, x))
+            recv(rx.at[n, g], xr_.at[n, g])
+        for k in range(4):
+            o = at_z[GROUPS[g][k]] * X + x
+            zero = jnp.zeros((32, 128), F32)
+            d0, d1 = None, None
+            for n in range(4):
+                a = prod_asks[0, o] if n == 0 else ib_s[peers_x[n - 1], 0, o]
+                v = slot[0, g, k] if n == 0 else rx[n - 1, g, k]
+                m0, m1 = jnp.where(a == 0, v, zero), jnp.where(a == 0, zero, v)
+                d0, d1 = (m0, m1) if n == 0 else (d0 + m0, d1 + m1)
+            dn[g, k, 0] = d0
+            dn[g, k, 1] = d1
+            if k == 0 and g == 0:
+                send(dn.at[0, 0], up.at[0], us.at[0], ur.at[0], to(z + 2, x))
+            if k >= 2:
+                send(dn.at[g, k], near.at[k - 2, g], ns.at[k - 2, g], nr.at[k - 2, g], to(z + (1 if k == 2 else -1), x))
+        if g == 0:
+            continue
+        recv(near.at[1, g - 1], nr.at[1, g - 1])
+        if g > 1:
+            recv(down.at[g - 2], dr.at[g - 2])
+        total = dn[g - 1, 1] + near[1, g - 1]
+        dsum[g - 1] = total if g == 1 else total + down[g - 2]
+        send(dsum.at[g - 1], down.at[g - 1], ds_.at[g - 1], dr.at[g - 1], to(z - 2, x))
+        recv(near.at[0, g - 1], nr.at[0, g - 1])
+        recv(up.at[g - 1], ur.at[g - 1])
+        usum[g - 1] = (dn[g, 0] + near[0, g - 1]) + up[g - 1]
+        send(usum.at[g - 1], up.at[g], us.at[g], ur.at[g], to(z + 2, x))
 
     for d in range(DP - 1):
         recv(rcnt.at[d], cr_.at[d])
@@ -276,10 +307,14 @@
         columns = pl.ds(pl.multiple_of(dp * 128, 128), 128)
         wflow_o[b] = w[b, :, columns].astype(F32) * total * (1.0 / 1024)
 
-    for j in (1, 3, 2):
-        recv(r2.at[j - 1], z2r.at[j - 1])
-    pflow_o[...] = (s2[0] + r2[0]) + (r2[1] + r2[2])
-    for c in sends:
+    recv(near.at[0, 3], nr.at[0, 3])
+    recv(near.at[1, 3], nr.at[1, 3])
+    own_flows = dn[3, 1] + (near[0, 3] + near[1, 3])
+    recv(down.at[2], dr.at[2])
+    own_flows = own_flows + down[2]
+    recv(up.at[3], ur.at[3])
+    pflow_o[...] = own_flows + up[3]
+    for c in sends[gathered:]:
         c.wait_send()
 
 
@@ -305,14 +340,17 @@
             V((64, 128), I32),
             V((2, 1024, 32), BF16),
             V((64, 32, 128), F32),
+            V((2, 32, 128), BF16),
             V((2, 1024, 128), BF16),
             V((2, 1024, 128), F32),
             V((65, 32, 128), F32),
-            V((64, 32, 128), F32),
+            V((4, 4, 4, 32, 128), F32),
             V((3, 4, 4, 32, 128), F32),
             V((4, 4, 2, 32, 128), F32),
-            V((3, 4, 2, 32, 128), F32),
+            V((2, 4, 2, 32, 128), F32),
             V((4, 2, 32, 128), F32),
+            V((3, 2, 32, 128), F32),
+            V((3, 2, 32, 128), F32),
             V((3, 2, 32, 128), F32),
             V((8, 2, 32, 128), F32),
             V((7, 2, 32, 128), F32),
@@ -321,7 +359,7 @@
             D((2,)),
             D((3,)), D((3,)),
             D((3, 4)), D((3, 4)),
-            D((3, 16)), D((3,)),
+            D((3, 16)), D((3,)), D((6,)), D((6,)), D((2,)),
             D((3,)), D((3,)),
             D((3,)), D((3,)),
             D((3, 4)), D((3,)),
@@ -330,7 +368,8 @@
             D((3, 4)), D((3,)),
             D((7,)), D((7,)),
             D((3, 4)), D((3, 4)),
-            D((3,)), D((3,)),
+            D((2, 4)), D((2, 4)),
+            D((4,)), D((4,)),
             D((3,)), D((3,)),
         ],
         compiler_params=pltpu.CompilerParams(

time: 77.1 us -> 72.3 us (0.938)
  the two profiles are of different devices: /device:TPU:32 before, /device:TPU:40 now
where the time goes in v2:
time: 72.3 us; the launch traced here: 71.9 us
  Pallas kernels  68.5 us (95%)
  local copies, waits for them, and re-layouts  2.77 us (4%)
    pallas_call x1, Pallas kernels, local(): pl.pallas_call(kernel, out_shape=(block, block, block), in_specs=[hbm] *...  68.5 us
    unnamed x7, local copies, waits for them, and re-layouts  2.77 us

profile of v2, /device:TPU:40, one launch (start us, length us, event | category | flops | bytes accessed | tf_op | source)
XLA Modules:
  0.0 71.9 jit_solution(1892839535349057710)
XLA Ops:
  0.6 68.5 %em_pass.1 = (f32[2,32,128]{2,1,0:T(8,128)}, f32[2,32,128]{2,1,0:T(8,128)}, f32[2,32,128]{2,1,0:T(8,128)}) custom-call(f32[2,32,128]{2,1,0:T(8,128)} %leaf_h.1, bf16[2,32,1024]{2,1,0:T(8,128)(2,1)} %w_h.1, f32[2,32,128]{2,1,0:T(8,128)} %upper_h.1, s32[1,64]{1,0:T(1,128)} %leaf_asks_h.1, s32[1,64]{1,0:T(1,128)} %prod_asks_h.1, s32[2,8]{1,0:T(2,128)} %prod_child_h.1, ...), custom_call_target="tpu_custom_call" | custom-call | tf_op jit(solution)/shard_map/em_pass/pallas_call | solution.py:326
  69.2 0.0 copy-start.1
  69.2 1.4 %copy.15 = f32[2,32,128]{2,1,0:T(8,128)} copy(f32[2,32,128]{2,1,0:T(8,128)} %get-tuple-element.6) | data formatting | bytes 65536
  70.6 0.0 copy-done.1
  70.6 0.0 copy-start
  70.6 0.6 copy.16
  71.2 0.2 copy-done
  71.3 0.6 copy.17
Async XLA Ops:
  69.2 1.4 %copy-start.1 = (f32[2,32,128]{2,1,0:T(8,128)S(1)}, f32[2,32,128]{2,1,0:T(8,128)}, u32[]{:S(2)}) copy-start(f32[2,32,128]{2,1,0:T(8,128)} %get-tuple-element.7) | copy-start | bytes 98308
  70.6 0.8 %copy-start = (f32[2,32,128]{2,1,0:T(8,128)S(1)}, f32[2,32,128]{2,1,0:T(8,128)}, u32[]{:S(2)}) copy-start(f32[2,32,128]{2,1,0:T(8,128)} %get-tuple-element.8) | copy-start | bytes 98308

commit v3 on v2

--- a/solution.py
+++ b/solution.py
@@ -97,12 +97,12 @@
     NEAR = ((0, 1), (1, -1), (2, 2))
     A = lambda p: lb.at[own(p), pl.ds(0, RA), :]
     for i, j in FAR:
+        send(ib.at[me], ib.at[me], i1s.at[i], i1r.at[i], to(z + 4 * j, x))
+    for i, j in FAR:
         send(A(me), A(me), a1s.at[i], a1r.at[i], to(z + 4 * j, x))
     for i, j in FAR:
         v = lb.at[own(me), pl.ds(RA, RB), :]
         send(v, v, b1s.at[i], b1r.at[i], to(z + 4 * j, x))
-    for i, j in FAR:
-        send(ib.at[me], ib.at[me], i1s.at[i], i1r.at[i], to(z + 4 * j, x))
     for i, d in NEAR:
         send(A(me), A(me), a2s.at[i, 0], a2r.at[i, 0], to(z + d, x))
 
@@ -143,6 +143,9 @@
     tcopy = pltpu.make_async_copy(tbl, tbl_s, lsem.at[0])
     tcopy.start()
 
+    for b in range(2):
+        wt[b] = jnp.transpose(w[b].astype(F32)).astype(BF16)
+
     for i, j in FAR:
         p = pos(z - 4 * j, x)
         recv(A(p), a1r.at[i])
@@ -179,8 +182,6 @@
     onward(0)
     relay(1, 3)
     onward(1)
-    relay(4, 8, 12)
-    onward(3)
     for n in range(3):
         xx = lax.rem(x + 3 - n, X)
         recv(Bc(xx, z), bxr.at[n])
@@ -188,12 +189,11 @@
         for m, d in NEAR:
             send(Bc(xx, z), Bc(xx, z), bzs.at[m, n + 1], bzr.at[m], to(z + d, x))
             send(Ic(xx, z), Ic(xx, z), izs.at[m, n + 1], izr.at[m], to(z + d, x))
+    relay(4, 8, 12)
+    onward(3)
     relay(5, 9, 13)
     onward(2)
     relay(7, 11, 15)
-
-    for b in range(2):
-        wt[b] = jnp.transpose(w[b].astype(F32)).astype(BF16)
 
     for n in range(3):
         recv(ib.at[pl.ds(0, 16)], izr.at[n])
@@ -318,12 +318,18 @@
         c.wait_send()
 
 
+def hand_over(a, b, c, a_o, b_o, c_o):
+    a_o[...] = a[...]
+    b_o[...] = b[...]
+    c_o[...] = c[...]
+
+
 def local(leaf_logp, weights, upper_flows, leaf_asks, prod_asks, prod_child, prod_valid, sum_child, sum_valid):
     D = pltpu.SemaphoreType.DMA
     block = jax.ShapeDtypeStruct((2, 32, 128), F32)
     vmem, hbm = pl.BlockSpec(memory_space=pltpu.VMEM), pl.BlockSpec(memory_space=pltpu.HBM)
     V, S = pltpu.VMEM, pltpu.SMEM
-    return pl.pallas_call(
+    made = pl.pallas_call(
         kernel,
         out_shape=(block, block, block),
         in_specs=[hbm] * 9,
@@ -379,6 +385,14 @@
     )(
         leaf_logp, weights, upper_flows, leaf_asks, prod_asks, prod_child, prod_valid, sum_child, sum_valid
     )
+    return pl.pallas_call(
+        hand_over,
+        out_shape=(block, block, block),
+        in_specs=[vmem] * 3,
+        out_specs=(vmem,) * 3,
+        compiler_params=pltpu.CompilerParams(vmem_limit_bytes=63 * 2**20),
+        name="hand_over",
+    )(*made)
 
 
 def solution(mesh):

time: 72.3 us -> 70.5 us (0.975)
  local copies, waits for them, and re-layouts: 2.77 us -> 0 us
  Pallas kernels: 68.5 us -> 69.7 us
    unnamed x7 -> x0, local copies, waits for them, and re-layouts: 2.77 us -> none
    pallas_call x0 -> x1, Pallas kernels: none -> 1.43 us  [local(): pl.pallas_call(hand_over, out_shape=(block, block, block), in_specs=[vmem...]
where the time goes in v3:
time: 70.5 us; the launch traced here: 70.3 us
  Pallas kernels  69.7 us (99%)
    pallas_call x1, Pallas kernels, local(): pl.pallas_call(kernel, out_shape=(block, block, block), in_specs=[hbm] *...  68.3 us
    pallas_call x1, Pallas kernels, local(): pl.pallas_call(hand_over, out_shape=(block, block, block), in_specs=[vmem...  1.43 us

profile of v3, /device:TPU:40, one launch (start us, length us, event | category | flops | bytes accessed | tf_op | source)
XLA Modules:
  0.0 70.3 jit_solution(3901101457696221462)
XLA Ops:
  0.6 68.3 %em_pass.1 = (f32[2,32,128]{2,1,0:T(8,128)}, f32[2,32,128]{2,1,0:T(8,128)}, f32[2,32,128]{2,1,0:T(8,128)}) custom-call(f32[2,32,128]{2,1,0:T(8,128)} %leaf_h.1, bf16[2,32,1024]{2,1,0:T(8,128)(2,1)} %w_h.1, f32[2,32,128]{2,1,0:T(8,128)} %upper_h.1, s32[1,64]{1,0:T(1,128)} %leaf_asks_h.1, s32[1,64]{1,0:T(1,128)} %prod_asks_h.1, s32[2,8]{1,0:T(2,128)} %prod_child_h.1, ...), custom_call_target="tpu_custom_call" | custom-call | tf_op jit(solution)/shard_map/em_pass/pallas_call | solution.py:332
  68.9 1.4 %hand_over.1 = (f32[2,32,128]{2,1,0:T(8,128)}, f32[2,32,128]{2,1,0:T(8,128)}, f32[2,32,128]{2,1,0:T(8,128)}) custom-call(f32[2,32,128]{2,1,0:T(8,128)} %get-tuple-element.6.a, f32[2,32,128]{2,1,0:T(8,128)} %get-tuple-element.7.b, f32[2,32,128]{2,1,0:T(8,128)} %get-tuple-element.8.c), custom_call_target="tpu_custom_call" | custom-call | tf_op jit(solution)/shard_map/hand_over/pallas_call | solution.py:388

commit v4 on v3

--- a/solution.py
+++ b/solution.py
@@ -224,7 +224,7 @@
             high = jnp.maximum(jnp.maximum(total[0:8], total[8:16]), jnp.maximum(total[16:24], total[24:32]))
             return jnp.maximum(top, jnp.where(sum_valid[b, e] > 0, high, -jnp.inf))
 
-        top = lax.fori_loop(0, 32, product, jnp.full((8, 128), -jnp.inf, F32), unroll=4)
+        top = lax.fori_loop(0, 32, product, jnp.full((8, 128), -jnp.inf, F32), unroll=8)
         colmax = jnp.max(top, axis=0, keepdims=True)
 
         def scale(e, _, b=b, colmax=colmax):
@@ -232,7 +232,7 @@
             scaled[b, pl.ds(pl.multiple_of(e * 32, 32), 32), :] = v.astype(BF16)
             return 0
 
-        lax.fori_loop(0, 32, scale, 0, unroll=4)
+        lax.fori_loop(0, 32, scale, 0, unroll=8)
         totals = jnp.dot(w[b], scaled[b], preferred_element_type=F32)
         loglik_o[b] = jnp.log(totals) + colmax
         ratios = (upper[b] / totals).astype(BF16)
@@ -245,7 +245,7 @@
         acc[i] = scaled[b, rows, :].astype(F32) * spread[b, rows, :] + acc[tbl_s[i, 0]]
         return 0
 
-    lax.fori_loop(0, 64, flow, 0, unroll=4)
+    lax.fori_loop(0, 64, flow, 0, unroll=8)
 
     at_z = {d: lax.rem(z + d + Z, Z) for d in range(-7, 9)}
     for g in range(4):

time: 70.5 us -> 70.3 us (level)
  no operation moved by 1% of the time
where the time goes in v4:
time: 70.3 us; the launch traced here: 70.1 us
  Pallas kernels  69.5 us (99%)
    pallas_call x1, Pallas kernels, local(): pl.pallas_call(kernel, out_shape=(block, block, block), in_specs=[hbm] *...  68.1 us
    pallas_call x1, Pallas kernels, local(): pl.pallas_call(hand_over, out_shape=(block, block, block), in_specs=[vmem...  1.43 us

profile of v4, /device:TPU:40, one launch (start us, length us, event | category | flops | bytes accessed | tf_op | source)
XLA Modules:
  0.0 70.1 jit_solution(17161221375285864570)
XLA Ops:
  0.6 68.1 %em_pass.1 = (f32[2,32,128]{2,1,0:T(8,128)}, f32[2,32,128]{2,1,0:T(8,128)}, f32[2,32,128]{2,1,0:T(8,128)}) custom-call(f32[2,32,128]{2,1,0:T(8,128)} %leaf_h.1, bf16[2,32,1024]{2,1,0:T(8,128)(2,1)} %w_h.1, f32[2,32,128]{2,1,0:T(8,128)} %upper_h.1, s32[1,64]{1,0:T(1,128)} %leaf_asks_h.1, s32[1,64]{1,0:T(1,128)} %prod_asks_h.1, s32[2,8]{1,0:T(2,128)} %prod_child_h.1, ...), custom_call_target="tpu_custom_call" | custom-call | tf_op jit(solution)/shard_map/em_pass/pallas_call | solution.py:332
  68.7 1.4 %hand_over.1 = (f32[2,32,128]{2,1,0:T(8,128)}, f32[2,32,128]{2,1,0:T(8,128)}, f32[2,32,128]{2,1,0:T(8,128)}) custom-call(f32[2,32,128]{2,1,0:T(8,128)} %get-tuple-element.6.a, f32[2,32,128]{2,1,0:T(8,128)} %get-tuple-element.7.b, f32[2,32,128]{2,1,0:T(8,128)} %get-tuple-element.8.c), custom_call_target="tpu_custom_call" | custom-call | tf_op jit(solution)/shard_map/hand_over/pallas_call | solution.py:388

commit v5 on v4

--- a/solution.py
+++ b/solution.py
@@ -255,16 +255,14 @@
         for n in (1, 2, 3):
             send(slot.at[n, g], rx.at[n - 1, g], xs.at[n - 1, g], xr_.at[n - 1, g], to(z, x + n))
 
-    for b in range(2):
-        counts = lax.dot_general(ratio[b], scaled[b], (((1,), (1,)), ((), ())), preferred_element_type=F32)
-        for d in range(DP):
-            cnt[d, b] = counts[:, d * 128 : (d + 1) * 128]
-    for d in range(1, DP):
-        other = lax.rem(dp + d, DP)
-        send(cnt.at[other], rcnt.at[d - 1], cs.at[d - 1], cr_.at[d - 1], {"dp": other})
-
-    for c in sends[:gathered]:
-        c.wait_send()
+    def count():
+        for b in range(2):
+            counts = lax.dot_general(ratio[b], scaled[b], (((1,), (1,)), ((), ())), preferred_element_type=F32)
+            for d in range(DP):
+                cnt[d, b] = counts[:, d * 128 : (d + 1) * 128]
+        for d in range(1, DP):
+            other = lax.rem(dp + d, DP)
+            send(cnt.at[other], rcnt.at[d - 1], cs.at[d - 1], cr_.at[d - 1], {"dp": other})
 
     peers_x = [pos(z, x + 3 - n) for n in range(3)]
     for g in range(4):
@@ -286,7 +284,10 @@
             if k >= 2:
                 send(dn.at[g, k], near.at[k - 2, g], ns.at[k - 2, g], nr.at[k - 2, g], to(z + (1 if k == 2 else -1), x))
         if g == 0:
+            count()
             continue
+        for c in sends[gathered * (g - 1) // 3 : gathered * g // 3]:
+            c.wait_send()
         recv(near.at[1, g - 1], nr.at[1, g - 1])
         if g > 1:
             recv(down.at[g - 2], dr.at[g - 2])
@@ -307,6 +308,9 @@
         columns = pl.ds(pl.multiple_of(dp * 128, 128), 128)
         wflow_o[b] = w[b, :, columns].astype(F32) * total * (1.0 / 1024)
 
+    late = len(sends) - 8
+    for c in sends[gathered:late]:
+        c.wait_send()
     recv(near.at[0, 3], nr.at[0, 3])
     recv(near.at[1, 3], nr.at[1, 3])
     own_flows = dn[3, 1] + (near[0, 3] + near[1, 3])
@@ -314,7 +318,7 @@
     own_flows = own_flows + down[2]
     recv(up.at[3], ur.at[3])
     pflow_o[...] = own_flows + up[3]
-    for c in sends[gathered:]:
+    for c in sends[late:]:
         c.wait_send()
 
 

time: 70.3 us -> 70.3 us (level)
  no operation moved by 1% of the time
where the time goes in v5:
time: 70.3 us; the launch traced here: 70.1 us
  Pallas kernels  69.5 us (99%)
    pallas_call x1, Pallas kernels, local(): pl.pallas_call(kernel, out_shape=(block, block, block), in_specs=[hbm] *...  68 us
    pallas_call x1, Pallas kernels, local(): pl.pallas_call(hand_over, out_shape=(block, block, block), in_specs=[vmem...  1.43 us

profile of v5, /device:TPU:40, one launch (start us, length us, event | category | flops | bytes accessed | tf_op | source)
XLA Modules:
  0.0 70.1 jit_solution(5991396362911887536)
XLA Ops:
  0.6 68.0 %em_pass.1 = (f32[2,32,128]{2,1,0:T(8,128)}, f32[2,32,128]{2,1,0:T(8,128)}, f32[2,32,128]{2,1,0:T(8,128)}) custom-call(f32[2,32,128]{2,1,0:T(8,128)} %leaf_h.1, bf16[2,32,1024]{2,1,0:T(8,128)(2,1)} %w_h.1, f32[2,32,128]{2,1,0:T(8,128)} %upper_h.1, s32[1,64]{1,0:T(1,128)} %leaf_asks_h.1, s32[1,64]{1,0:T(1,128)} %prod_asks_h.1, s32[2,8]{1,0:T(2,128)} %prod_child_h.1, ...), custom_call_target="tpu_custom_call" | custom-call | tf_op jit(solution)/shard_map/em_pass/pallas_call | solution.py:336
  68.7 1.4 %hand_over.1 = (f32[2,32,128]{2,1,0:T(8,128)}, f32[2,32,128]{2,1,0:T(8,128)}, f32[2,32,128]{2,1,0:T(8,128)}) custom-call(f32[2,32,128]{2,1,0:T(8,128)} %get-tuple-element.6.a, f32[2,32,128]{2,1,0:T(8,128)} %get-tuple-element.7.b, f32[2,32,128]{2,1,0:T(8,128)} %get-tuple-element.8.c), custom_call_target="tpu_custom_call" | custom-call | tf_op jit(solution)/shard_map/hand_over/pallas_call | solution.py:392
